TPU v7x, 32 devices: a whole 2x2x4 slice. The times are simulated.
32 devices in a mesh: groups: 2 (over y), feat: 8 (over z, core), tok: 2 (over x).
Axes of the slice: x: 2, y: 2, z: 4, core: 2. Of those that a mesh axis runs over, the one named last changes fastest.
Arguments:
- tokens: bfloat16 [1024, 4096], P(('groups', 'feat'), 'tok'), parts along dimension 0, may hold values from -6 to 6
- out_grad: bfloat16 [1024, 4096], P(('groups', 'feat'), 'tok'), parts along dimension 0, may hold values from -0.75 to 0.75
- gate_weight: bfloat16 [4096, 14336], P('tok', 'feat'), may hold values from -0.09375 to 0.09375
- up_weight: bfloat16 [4096, 14336], P('tok', 'feat'), may hold values from -0.09375 to 0.09375
- down_weight: bfloat16 [14336, 4096], P('feat', 'tok'), may hold values from -0.046875 to 0.046875
Outputs:
- grad_gate: bfloat16 [8192, 14336], P(('groups', 'tok'), 'feat'), parts along dimension 0
- grad_up: bfloat16 [8192, 14336], P(('groups', 'tok'), 'feat'), parts along dimension 0
- grad_down: bfloat16 [28672, 4096], P(('groups', 'feat'), 'tok'), parts along dimension 0
There are 2 independent parts, one for each index of `groups`. A program takes and returns all parts, laid end to end along the dimension named above; an argument that names none is the same for every part. Nothing has to cross between parts.
All inputs are finite; a program needn't handle non-finite values.
Results may differ from a plain program's by a relative error of at most 0.005.
Values may be sent and summed in bfloat16 or wider, within the bound.
A program may use at most 128 MiB of HBM per device.

v0:
```python
import jax
import jax.numpy as jnp
from jax import lax
from jax.sharding import PartitionSpec as P


def contract_rows(left, right):
    return lax.dot_general(
        left, right, (((0,), (0,)), ((), ())), preferred_element_type=jnp.float32
    )


def swiglu_parts(gate, up, grad_hidden):
    sigmoid_gate = jax.nn.sigmoid(gate)
    activated = gate * sigmoid_gate
    hidden = (activated * up).astype(jnp.bfloat16)
    gate_delta = (grad_hidden * up * sigmoid_gate * (1.0 + gate * (1.0 - sigmoid_gate))).astype(
        jnp.bfloat16
    )
    up_delta = (grad_hidden * activated).astype(jnp.bfloat16)
    return (hidden, gate_delta, up_delta)


def shards(tokens, out_grad, gate_weight, up_weight, down_weight):
    token_rows, grad_rows = (
        lax.all_gather(tokens, "feat", axis=0, tiled=True),
        lax.all_gather(out_grad, "feat", axis=0, tiled=True),
    )
    gate_part = jnp.dot(token_rows, gate_weight, preferred_element_type=jnp.float32)
    up_part = jnp.dot(token_rows, up_weight, preferred_element_type=jnp.float32)
    hidden_part = lax.dot_general(
        grad_rows, down_weight, (((1,), (1,)), ((), ())), preferred_element_type=jnp.float32
    )
    gate, up = (
        lax.psum_scatter(gate_part, "tok", scatter_dimension=0, tiled=True),
        lax.psum_scatter(up_part, "tok", scatter_dimension=0, tiled=True),
    )
    grad_hidden = lax.psum_scatter(hidden_part, "tok", scatter_dimension=0, tiled=True)
    hidden, gate_delta, up_delta = swiglu_parts(gate, up, grad_hidden)
    hidden, gate_delta, up_delta = (
        lax.all_gather(hidden, "tok", axis=0, tiled=True),
        lax.all_gather(gate_delta, "tok", axis=0, tiled=True),
        lax.all_gather(up_delta, "tok", axis=0, tiled=True),
    )
    grad_gate = contract_rows(token_rows, gate_delta).astype(jnp.bfloat16)
    grad_up = contract_rows(token_rows, up_delta).astype(jnp.bfloat16)
    grad_down = contract_rows(hidden, grad_rows).astype(jnp.bfloat16)
    return (grad_gate, grad_up, grad_down)


def solution(mesh):
    return jax.shard_map(
        shards,
        mesh=mesh,
        in_specs=(
            P(("groups", "feat"), "tok"),
            P(("groups", "feat"), "tok"),
            P("tok", "feat"),
            P("tok", "feat"),
            P("feat", "tok"),
        ),
        out_specs=(
            P(("groups", "tok"), "feat"),
            P(("groups", "tok"), "feat"),
            P(("groups", "feat"), "tok"),
        ),
        check_vma=False,
    )
```

profile of v0, /device:TPU:0, one launch (start us, length us, event | category | flops | bytes accessed | tf_op | source)
XLA Modules:
  0.0 340.8 jit_solution(12979034745607124488)
XLA Ops:
  7.2 0.0 all-gather.8.cloned.1.call-start
  7.2 0.7 all-gather.8.cloned.1.call-update
  7.9 0.0 all-gather.6.cloned.1.call-start
  7.9 0.7 all-gather.6.cloned.1.call-update
  8.6 0.0 reduce-scatter.6.cloned.1.call-start
  8.7 32.7 %all-gather.8.cloned.1.call-done = bf16[512,2048]{1,0:T(8,128)(2,1)} async-done(((bf16[64,2048]{1,0:T(8,128)(2,1)}), bf16[512,2048]{1,0:T(8,128)(2,1)}) %all-gather.8.cloned.1.call-update) | async-done | bytes 2097168 | tf_op jit(solution)/shard_map/all_gather | solution.py:26
  41.4 9.5 %fusion.4 = f32[512,1792]{1,0:T(8,128)} fusion(bf16[512,2048]{1,0:T(8,128)(2,1)} %all-gather.8.cloned.1.call-done, bf16[2048,1792]{1,0:T(8,128)(2,1)} %param.8), kind=kOutput, calls=%fused_computation.11 | convolution fusion | flops 3758096384 | bytes 13107200 | tf_op jit(solution)/shard_map/dot_general | solution.py:30
  50.9 0.0 copy-start.1
  50.9 0.0 reduce-scatter.6.cloned.1.call-update
  51.0 0.0 reduce-scatter.8.cloned.1.call-start
  51.0 1.5 copy-done.1
  52.5 8.9 %fusion.5 = f32[512,1792]{1,0:T(8,128)} fusion(bf16[512,2048]{1,0:T(8,128)(2,1)S(1)} %copy-done.1, bf16[2048,1792]{1,0:T(8,128)(2,1)} %param.7), kind=kOutput, calls=%fused_computation.12 | convolution fusion | flops 3758096384 | bytes 13107200 | tf_op jit(solution)/shard_map/dot_general | solution.py:29
  61.4 0.0 reduce-scatter.8.cloned.1.call-update
  61.4 0.0 reduce-scatter.4.cloned.1.call-start
  61.5 10.2 %all-gather.6.cloned.1.call-done = bf16[512,2048]{1,0:T(8,128)(2,1)} async-done(((bf16[64,2048]{1,0:T(8,128)(2,1)}), bf16[512,2048]{1,0:T(8,128)(2,1)}) %all-gather.6.cloned.1.call-update) | async-done | bytes 2097168 | tf_op jit(solution)/shard_map/all_gather | solution.py:27
  71.7 9.9 %fusion.3 = f32[512,1792]{1,0:T(8,128)} fusion(bf16[512,2048]{1,0:T(8,128)(2,1)} %all-gather.6.cloned.1.call-done, bf16[1792,2048]{1,0:T(8,128)(2,1)} %param.9), kind=kOutput, calls=%fused_computation.10 | convolution fusion | flops 3758096384 | bytes 13107200 | tf_op jit(solution)/shard_map/dot_general | solution.py:31
  81.5 0.0 reduce-scatter.4.cloned.1.call-update
  81.6 0.0 all-gather.12.cloned.1.call-start
  81.6 41.5 %reduce-scatter.6.cloned.1.call-done = f32[256,1792]{1,0:T(8,128)} async-done(((f32[512,1792]{1,0:T(8,128)}), f32[256,1792]{1,0:T(8,128)}) %reduce-scatter.6.cloned.1.call-update) | async-done | bytes 1835024 | tf_op jit(solution)/shard_map/reduce_scatter | solution.py:36
  123.1 51.9 %reduce-scatter.8.cloned.1.call-done = f32[256,1792]{1,0:T(8,128)} async-done(((f32[512,1792]{1,0:T(8,128)}), f32[256,1792]{1,0:T(8,128)}) %reduce-scatter.8.cloned.1.call-update) | async-done | bytes 1835024 | tf_op jit(solution)/shard_map/reduce_scatter | solution.py:35
  175.0 51.8 %reduce-scatter.4.cloned.1.call-done = f32[256,1792]{1,0:T(8,128)} async-done(((f32[512,1792]{1,0:T(8,128)}), f32[256,1792]{1,0:T(8,128)}) %reduce-scatter.4.cloned.1.call-update) | async-done | bytes 1835024 | tf_op jit(solution)/shard_map/reduce_scatter | solution.py:38
  226.8 5.0 %multiply_convert_fusion = (bf16[256,1792]{1,0:T(8,128)(2,1)}, bf16[256,1792]{1,0:T(8,128)(2,1)}, bf16[256,1792]{1,0:T(8,128)(2,1)}) fusion(f32[256,1792]{1,0:T(8,128)} %reduce-scatter.6.cloned.1.call-done, f32[256,1792]{1,0:T(8,128)} %reduce-scatter.8.cloned.1.call-done, f32[256,1792]{1,0:T(8,128)} %reduce-scatter.4.cloned.1.call-done), kind=kLoop, calls=%fused_computation.5 | loop fusion | flops 6881280 | bytes 8257536 | tf_op jit(solution)/shard_map/convert_element_type | solution.py:16
  231.9 0.0 all-gather.12.cloned.1.call-update
  231.9 0.0 all-gather.10.cloned.1.call-start
  231.9 0.7 all-gather.10.cloned.1.call-update
  232.6 0.2 all-gather.14.cloned.1.call-start
  232.9 0.5 all-gather.14.cloned.1.call-update
  233.4 28.8 %all-gather.12.cloned.1.call-done = bf16[512,1792]{1,0:T(8,128)(2,1)} async-done(((bf16[256,1792]{1,0:T(8,128)(2,1)}), bf16[512,1792]{1,0:T(8,128)(2,1)}) %all-gather.12.cloned.1.call-update) | async-done | bytes 1835024 | tf_op jit(solution)/shard_map/all_gather | solution.py:43
  262.2 7.5 %fusion.1 = bf16[2048,1792]{0,1:T(8,128)(2,1)} fusion(bf16[512,1792]{1,0:T(8,128)(2,1)} %all-gather.12.cloned.1.call-done, bf16[512,2048]{1,0:T(8,128)(2,1)S(1)} %copy-done.1), kind=kOutput, calls=%fused_computation.4 | convolution fusion | flops 3761766400 | bytes 11272192 | tf_op jit(solution)/shard_map/dot_general | solution.py:8
  269.8 10.0 %copy.9 = bf16[2048,1792]{1,0:T(8,128)(2,1)} copy(bf16[2048,1792]{0,1:T(8,128)(2,1)} %fusion.1) | data formatting | bytes 14680064
  279.8 14.8 %all-gather.10.cloned.1.call-done = bf16[512,1792]{1,0:T(8,128)(2,1)} async-done(((bf16[256,1792]{1,0:T(8,128)(2,1)}), bf16[512,1792]{1,0:T(8,128)(2,1)}) %all-gather.10.cloned.1.call-update) | async-done | bytes 1835024 | tf_op jit(solution)/shard_map/all_gather | solution.py:42
  294.6 7.6 %fusion = bf16[2048,1792]{0,1:T(8,128)(2,1)} fusion(bf16[512,1792]{1,0:T(8,128)(2,1)} %all-gather.10.cloned.1.call-done, bf16[512,2048]{1,0:T(8,128)(2,1)S(1)} %copy-done.1), kind=kOutput, calls=%fused_computation.3 | convolution fusion | flops 3761766400 | bytes 11272192 | tf_op jit(solution)/shard_map/dot_general | solution.py:8
  302.2 0.0 copy-start
  302.2 10.2 %copy.8 = bf16[2048,1792]{1,0:T(8,128)(2,1)} copy(bf16[2048,1792]{0,1:T(8,128)(2,1)} %fusion) | data formatting | bytes 14680064
  312.3 14.1 %all-gather.14.cloned.1.call-done = bf16[512,1792]{1,0:T(8,128)(2,1)} async-done(((bf16[256,1792]{1,0:T(8,128)(2,1)}), bf16[512,1792]{1,0:T(8,128)(2,1)}) %all-gather.14.cloned.1.call-update) | async-done | bytes 1835024 | tf_op jit(solution)/shard_map/all_gather | solution.py:41
  326.4 0.0 copy-done
  326.4 7.6 %convolution_convert_fusion = bf16[1792,2048]{1,0:T(8,128)(2,1)} fusion(bf16[512,1792]{1,0:T(8,128)(2,1)} %all-gather.14.cloned.1.call-done, bf16[512,2048]{1,0:T(8,128)(2,1)S(1)} %copy-done), kind=kOutput, calls=%fused_computation | convolution fusion | flops 3761766400 | bytes 11272192 | tf_op jit(solution)/shard_map/dot_general | solution.py:8
Async XLA Ops:
  7.2 34.3 %all-gather.8.cloned.1.call-start = ((), (), s32[]{:S(2)}) async-start(), calls=%async_computation.5 | async-start | bytes 2359296 | tf_op jit(solution)/shard_map/all_gather | solution.py:26
  7.9 63.8 %all-gather.6.cloned.1.call-start = ((), (), s32[]{:S(2)}) async-start(), calls=%async_computation.3 | async-start | bytes 2359296 | tf_op jit(solution)/shard_map/all_gather | solution.py:27
  8.6 114.5 %reduce-scatter.6.cloned.1.call-start = ((), (), s32[]{:S(2)}) async-start(), calls=%async_computation.6 | async-start | bytes 5505024 | tf_op jit(solution)/shard_map/reduce_scatter | solution.py:36
  50.9 1.6 copy-start.1
  51.0 124.1 %reduce-scatter.8.cloned.1.call-start = ((), (), s32[]{:S(2)}) async-start(), calls=%async_computation.7 | async-start | bytes 5505024 | tf_op jit(solution)/shard_map/reduce_scatter | solution.py:35
  61.4 165.4 %reduce-scatter.4.cloned.1.call-start = ((), (), s32[]{:S(2)}) async-start(), calls=%async_computation.4 | async-start | bytes 5505024 | tf_op jit(solution)/shard_map/reduce_scatter | solution.py:38
  81.6 180.6 %all-gather.12.cloned.1.call-start = ((), (), s32[]{:S(2)}) async-start(), calls=%async_computation.9 | async-start | bytes 2752512 | tf_op jit(solution)/shard_map/all_gather | solution.py:43
  231.9 62.7 %all-gather.10.cloned.1.call-start = ((), (), s32[]{:S(2)}) async-start(), calls=%async_computation.8 | async-start | bytes 2752512 | tf_op jit(solution)/shard_map/all_gather | solution.py:42
  232.6 93.8 %all-gather.14.cloned.1.call-start = ((), (), s32[]{:S(2)}) async-start(), calls=%async_computation.10 | async-start | bytes 2752512 | tf_op jit(solution)/shard_map/all_gather | solution.py:41
  302.2 24.3 %copy-start = (bf16[512,2048]{1,0:T(8,128)(2,1)S(1)}, bf16[512,2048]{1,0:T(8,128)(2,1)}, u32[]{:S(2)}) copy-start(bf16[512,2048]{1,0:T(8,128)(2,1)} %all-gather.6.cloned.1.call-done) | copy-start | bytes 6291460
Sparse Core Ops, SparseCore 0:
  9.6 31.7 all-gather.7
  43.0 28.5 all-gather.5
  74.5 48.5 reduce-scatter.5
  125.9 49.0 reduce-scatter.7
  177.7 49.0 reduce-scatter.3
  232.0 30.1 all-gather.11
  264.4 30.1 all-gather.9
  296.2 30.1 all-gather.13
where the time goes:
time: 342 us; the launch traced here: 341 us
  waiting for transfers between devices  248 us (73%)
  matrix products  50.9 us (15%)
  local copies, waits for them, and re-layouts  21.7 us (6%)
  between operations  14.1 us (4%)
  other arithmetic  5.03 us (1%)
    reduce_scatter x1, waiting for transfers between devices, shards(): lax.psum_scatter(gate_part, 'tok', scatter_dimension=0, tiled=True)  51.9 us
    reduce_scatter x1, waiting for transfers between devices, shards(): lax.psum_scatter(hidden_part, 'tok', scatter_dimension=0, tiled=True)  51.8 us
    reduce_scatter x1, waiting for transfers between devices, shards(): lax.psum_scatter(up_part, 'tok', scatter_dimension=0, tiled=True)  41.5 us
    all_gather x1, waiting for transfers between devices, shards(): lax.all_gather(tokens, 'feat', axis=0, tiled=True)  32.7 us
    all_gather x1, waiting for transfers between devices, shards(): lax.all_gather(up_delta, 'tok', axis=0, tiled=True)  28.8 us
    dot_general x3, matrix products, contract_rows(): lax.dot_general(left, right, (((0,), (0,)), ((), ())), preferred_element_...  22.7 us
    unnamed x6, local copies, waits for them, and re-layouts  21.7 us
    all_gather x1, waiting for transfers between devices, shards(): lax.all_gather(gate_delta, 'tok', axis=0, tiled=True)  14.8 us
  transfers between devices with their start and end apart: 8, of which 8 were waited for; matrix products, arithmetic and copies ran while one was open for 19% of the time, Pallas kernels for 0%

commit v1 on v0

--- a/solution.py
+++ b/solution.py
@@ -2,6 +2,28 @@
 import jax.numpy as jnp
 from jax import lax
 from jax.sharding import PartitionSpec as P
+
+
+def in_order(blocks, dim):
+    blocks = jnp.moveaxis(blocks, 0, dim)
+    shape = blocks.shape
+    return blocks.reshape(*shape[:dim], shape[dim] * shape[dim + 1], *shape[dim + 2 :])
+
+
+def gather_around(shard, axis, dim):
+    size = lax.axis_size(axis)
+    pairs = [(i, (i + 1) % size) for i in range(size)]
+    back = [(b, a) for a, b in pairs]
+    lower, upper = ([], [])
+    for step in range(size - 1):
+        if step % 2 == 0:
+            lower.append(lax.ppermute(lower[-1] if lower else shard, axis, pairs))
+        else:
+            upper.append(lax.ppermute(upper[-1] if upper else shard, axis, back))
+    blocks = jnp.stack([*lower[::-1], shard, *upper])
+    shift = lax.axis_index(axis) - len(lower)
+    blocks = blocks[(jnp.arange(size) - shift) % size]
+    return in_order(blocks, dim)
 
 
 def contract_rows(left, right):
@@ -24,7 +46,7 @@
 def shards(tokens, out_grad, gate_weight, up_weight, down_weight):
     token_rows, grad_rows = (
         lax.all_gather(tokens, "feat", axis=0, tiled=True),
-        lax.all_gather(out_grad, "feat", axis=0, tiled=True),
+        gather_around(out_grad, "feat", 0),
     )
     gate_part = jnp.dot(token_rows, gate_weight, preferred_element_type=jnp.float32)
     up_part = jnp.dot(token_rows, up_weight, preferred_element_type=jnp.float32)

time: 342 us -> 325 us (0.950)
  waiting for transfers between devices: 248 us -> 215 us
  starting transfers between devices: 0.5 us -> 11.7 us
  local copies, waits for them, and re-layouts: 21.7 us -> 25.9 us
    reduce_scatter x1, waiting for transfers between devices: 51.8 us -> 19 us  [shards(): lax.psum_scatter(hidden_part, 'tok', scatter_dimension=0, tiled=True)]
    ppermute x0 -> x7, waiting for transfers between devices: none -> 25.5 us  [the longest x4 25.5 us: gather_around(): lower.append(lax.ppermute(lower[-1] if lower else shard, axis, pairs))]
    all_gather x1, waiting for transfers between devices: 32.7 us -> 8.57 us  [shards(): lax.all_gather(tokens, 'feat', axis=0, tiled=True)]
    all_gather x1, waiting for transfers between devices: 28.8 us -> 14.7 us  [shards(): lax.all_gather(up_delta, 'tok', axis=0, tiled=True)]
    all_gather x1, waiting for transfers between devices: 14.8 us -> 28.6 us  [shards(): lax.all_gather(gate_delta, 'tok', axis=0, tiled=True)]
    ppermute x0 -> x7, starting transfers between devices: none -> 11.2 us  [the longest x3 10.7 us: gather_around(): upper.append(lax.ppermute(upper[-1] if upper else shard, axis, back))]
    reduce_scatter x1, waiting for transfers between devices: 41.5 us -> 51.8 us  [shards(): lax.psum_scatter(up_part, 'tok', scatter_dimension=0, tiled=True)]
    all_gather x1 -> x0, waiting for transfers between devices: 10.2 us -> none  [shards(): lax.all_gather(out_grad, 'feat', axis=0, tiled=True)]
  transfers between devices with their start and end apart: 8 -> 14, of which waited for: 8 -> 11; matrix products, arithmetic and copies ran while one was open for 19% -> 21% of each run, Pallas kernels for 0% -> 0%
where the time goes in v1:
time: 325 us; the launch traced here: 324 us
  waiting for transfers between devices  215 us (66%)
  matrix products  50.6 us (16%)
  local copies, waits for them, and re-layouts  25.9 us (8%)
  between operations  15.7 us (5%)
  starting transfers between devices  11.7 us (4%)
  other arithmetic  5.05 us (2%)
    reduce_scatter x1, waiting for transfers between devices, shards(): lax.psum_scatter(up_part, 'tok', scatter_dimension=0, tiled=True)  51.8 us
    reduce_scatter x1, waiting for transfers between devices, shards(): lax.psum_scatter(gate_part, 'tok', scatter_dimension=0, tiled=True)  51.7 us
    all_gather x1, waiting for transfers between devices, shards(): lax.all_gather(gate_delta, 'tok', axis=0, tiled=True)  28.6 us
    ppermute x4, waiting for transfers between devices, gather_around(): lower.append(lax.ppermute(lower[-1] if lower else shard, axis, pairs))  25.5 us
    unnamed x17, local copies, waits for them, and re-layouts  23.9 us
    dot_general x3, matrix products, contract_rows(): lax.dot_general(left, right, (((0,), (0,)), ((), ())), preferred_element_...  22.7 us
    reduce_scatter x1, waiting for transfers between devices, shards(): lax.psum_scatter(hidden_part, 'tok', scatter_dimension=0, tiled=True)  19 us
    all_gather x1, waiting for transfers between devices, shards(): lax.all_gather(up_delta, 'tok', axis=0, tiled=True)  14.7 us
  transfers between devices with their start and end apart: 14, of which 11 were waited for; matrix products, arithmetic and copies ran while one was open for 21% of the time, Pallas kernels for 0%

profile of v1, /device:TPU:0, one launch (start us, length us, event | category | flops | bytes accessed | tf_op | source)
XLA Modules:
  0.0 324.2 jit_solution(15252756857739211305)
XLA Ops:
  8.0 0.0 copy-start.1
  8.0 0.0 all-gather.5.cloned.1.call-start
  8.1 0.5 collective-permute-start
  8.6 8.3 %collective-permute-done = bf16[64,2048]{1,0:T(8,128)(2,1)S(1)} collective-permute-done((bf16[64,2048]{1,0:T(8,128)(2,1)}, bf16[64,2048]{1,0:T(8,128)(2,1)S(1)}, u32[]{:S(2)}, u32[]{:S(2)}) %collective-permute-start) | collective-permute-done | bytes 262176 | tf_op jit(solution)/shard_map/ppermute | solution.py:20
  16.9 0.0 collective-permute-start.1
  16.9 3.5 %collective-permute-start.4 = (bf16[64,2048]{1,0:T(8,128)(2,1)}, bf16[64,2048]{1,0:T(8,128)(2,1)S(1)}, u32[]{:S(2)}, u32[]{:S(2)}) collective-permute-start(bf16[64,2048]{1,0:T(8,128)(2,1)} %param.6), channel_id=1, source_target_pairs={{2,0},{4,2},{6,4},{8,6},{10,8},{12,10},{14,12},{0,14},{3,1},{5,3},... | collective-permute-start | bytes 786440 | tf_op jit(solution)/shard_map/ppermute | solution.py:22
  20.4 5.9 %collective-permute-done.1 = bf16[64,2048]{1,0:T(8,128)(2,1)S(1)} collective-permute-done((bf16[64,2048]{1,0:T(8,128)(2,1)S(1)}, bf16[64,2048]{1,0:T(8,128)(2,1)S(1)}, u32[]{:S(2)}, u32[]{:S(2)}) %collective-permute-start.1) | collective-permute-done | bytes 262176 | tf_op jit(solution)/shard_map/ppermute | solution.py:20
  26.3 0.0 collective-permute-start.2
  26.3 0.0 collective-permute-done.4
  26.4 3.5 %collective-permute-start.5 = (bf16[64,2048]{1,0:T(8,128)(2,1)S(1)}, bf16[64,2048]{1,0:T(8,128)(2,1)S(1)}, u32[]{:S(2)}, u32[]{:S(2)}) collective-permute-start(bf16[64,2048]{1,0:T(8,128)(2,1)S(1)} %collective-permute-done.4), channel_id=1, source_target_pairs={{2,0},{4,2},{6,4},{8,6},{10,8},{12,10},{14,12},{0,14},{3,1},{5,3},... | collective-permute-start | bytes 786440 | tf_op jit(solution)/shard_map/ppermute | solution.py:22
  29.9 6.3 %collective-permute-done.2 = bf16[64,2048]{1,0:T(8,128)(2,1)S(1)} collective-permute-done((bf16[64,2048]{1,0:T(8,128)(2,1)S(1)}, bf16[64,2048]{1,0:T(8,128)(2,1)S(1)}, u32[]{:S(2)}, u32[]{:S(2)}) %collective-permute-start.2) | collective-permute-done | bytes 262176 | tf_op jit(solution)/shard_map/ppermute | solution.py:20
  36.2 0.0 copy-start.2
  36.2 0.0 collective-permute-start.3
  36.2 0.0 all-gather.5.cloned.1.call-update
  36.2 0.0 reduce-scatter.4.cloned.1.call-start
  36.3 0.0 collective-permute-done.5
  36.3 3.6 %collective-permute-start.6 = (bf16[64,2048]{1,0:T(8,128)(2,1)S(1)}, bf16[64,2048]{1,0:T(8,128)(2,1)S(1)}, u32[]{:S(2)}, u32[]{:S(2)}) collective-permute-start(bf16[64,2048]{1,0:T(8,128)(2,1)S(1)} %collective-permute-done.5), channel_id=1, source_target_pairs={{2,0},{4,2},{6,4},{8,6},{10,8},{12,10},{14,12},{0,14},{3,1},{5,3},... | collective-permute-start | bytes 786440 | tf_op jit(solution)/shard_map/ppermute | solution.py:22
  39.9 0.0 copy-done.2
  39.9 4.9 %collective-permute-done.3 = bf16[64,2048]{1,0:T(8,128)(2,1)} collective-permute-done((bf16[64,2048]{1,0:T(8,128)(2,1)S(1)}, bf16[64,2048]{1,0:T(8,128)(2,1)}, u32[]{:S(2)}, u32[]{:S(2)}) %collective-permute-start.3) | collective-permute-done | bytes 262176 | tf_op jit(solution)/shard_map/ppermute | solution.py:20
  44.8 1.0 bitcast_dynamic-update-slice_fusion.7
  45.8 1.0 bitcast_dynamic-update-slice_fusion.6
  46.9 0.0 copy-done.1
  47.0 0.0 collective-permute-done.6
  47.0 2.0 gather_fusion
  49.0 9.6 %fusion.5 = f32[512,1792]{1,0:T(8,128)} fusion(bf16[512,2048]{1,0:T(8,128)(2,1)} %bitcast.35, bf16[1792,2048]{1,0:T(8,128)(2,1)} %param.9), kind=kOutput, calls=%fused_computation.26 | convolution fusion | flops 3758096384 | bytes 13107200 | tf_op jit(solution)/shard_map/dot_general | solution.py:53
  58.6 0.0 reduce-scatter.4.cloned.1.call-update
  58.7 0.0 reduce-scatter.6.cloned.1.call-start
  58.7 8.6 %all-gather.5.cloned.1.call-done = bf16[512,2048]{1,0:T(8,128)(2,1)} async-done(((bf16[64,2048]{1,0:T(8,128)(2,1)}), bf16[512,2048]{1,0:T(8,128)(2,1)}) %all-gather.5.cloned.1.call-update) | async-done | bytes 2097168 | tf_op jit(solution)/shard_map/all_gather | solution.py:48
  67.3 9.5 %fusion.6 = f32[512,1792]{1,0:T(8,128)} fusion(bf16[512,2048]{1,0:T(8,128)(2,1)} %all-gather.5.cloned.1.call-done, bf16[2048,1792]{1,0:T(8,128)(2,1)} %param.8), kind=kOutput, calls=%fused_computation.27 | convolution fusion | flops 3758096384 | bytes 13107200 | tf_op jit(solution)/shard_map/dot_general | solution.py:52
  76.8 0.0 copy-start.3
  76.8 0.0 reduce-scatter.6.cloned.1.call-update
  76.8 0.0 reduce-scatter.8.cloned.1.call-start
  76.9 1.6 copy-done.3
  78.5 8.9 %fusion.7 = f32[512,1792]{1,0:T(8,128)} fusion(bf16[512,2048]{1,0:T(8,128)(2,1)S(1)} %copy-done.3, bf16[2048,1792]{1,0:T(8,128)(2,1)} %param.7), kind=kOutput, calls=%fused_computation.28 | convolution fusion | flops 3758096384 | bytes 13107200 | tf_op jit(solution)/shard_map/dot_general | solution.py:51
  87.3 0.0 reduce-scatter.8.cloned.1.call-update
  87.4 0.2 all-gather.7.cloned.1.call-start
  87.6 19.0 %reduce-scatter.4.cloned.1.call-done = f32[256,1792]{1,0:T(8,128)} async-done(((f32[512,1792]{1,0:T(8,128)}), f32[256,1792]{1,0:T(8,128)}) %reduce-scatter.4.cloned.1.call-update) | async-done | bytes 1835024 | tf_op jit(solution)/shard_map/reduce_scatter | solution.py:60
  106.6 51.8 %reduce-scatter.6.cloned.1.call-done = f32[256,1792]{1,0:T(8,128)} async-done(((f32[512,1792]{1,0:T(8,128)}), f32[256,1792]{1,0:T(8,128)}) %reduce-scatter.6.cloned.1.call-update) | async-done | bytes 1835024 | tf_op jit(solution)/shard_map/reduce_scatter | solution.py:58
  158.4 51.7 %reduce-scatter.8.cloned.1.call-done = f32[256,1792]{1,0:T(8,128)} async-done(((f32[512,1792]{1,0:T(8,128)}), f32[256,1792]{1,0:T(8,128)}) %reduce-scatter.8.cloned.1.call-update) | async-done | bytes 1835024 | tf_op jit(solution)/shard_map/reduce_scatter | solution.py:57
  210.1 5.0 %multiply_convert_fusion = (bf16[256,1792]{1,0:T(8,128)(2,1)}, bf16[256,1792]{1,0:T(8,128)(2,1)}, bf16[256,1792]{1,0:T(8,128)(2,1)}) fusion(f32[256,1792]{1,0:T(8,128)} %reduce-scatter.6.cloned.1.call-done, f32[256,1792]{1,0:T(8,128)} %reduce-scatter.8.cloned.1.call-done, f32[256,1792]{1,0:T(8,128)} %reduce-scatter.4.cloned.1.call-done), kind=kLoop, calls=%fused_computation.6 | loop fusion | flops 6881280 | bytes 8257536 | tf_op jit(solution)/shard_map/convert_element_type | solution.py:38
  215.1 0.0 all-gather.7.cloned.1.call-update
  215.1 0.0 all-gather.9.cloned.1.call-start
  215.2 0.7 all-gather.9.cloned.1.call-update
  215.9 0.0 all-gather.11.cloned.1.call-start
  215.9 0.7 all-gather.11.cloned.1.call-update
  216.6 28.6 %all-gather.7.cloned.1.call-done = bf16[512,1792]{1,0:T(8,128)(2,1)} async-done(((bf16[256,1792]{1,0:T(8,128)(2,1)}), bf16[512,1792]{1,0:T(8,128)(2,1)}) %all-gather.7.cloned.1.call-update) | async-done | bytes 1835024 | tf_op jit(solution)/shard_map/all_gather | solution.py:64
  245.3 7.5 %fusion = bf16[2048,1792]{0,1:T(8,128)(2,1)} fusion(bf16[512,1792]{1,0:T(8,128)(2,1)} %all-gather.7.cloned.1.call-done, bf16[512,2048]{1,0:T(8,128)(2,1)S(1)} %copy-done.3), kind=kOutput, calls=%fused_computation.4 | convolution fusion | flops 3761766400 | bytes 11272192 | tf_op jit(solution)/shard_map/dot_general | solution.py:30
  252.8 10.0 %copy.8 = bf16[2048,1792]{1,0:T(8,128)(2,1)} copy(bf16[2048,1792]{0,1:T(8,128)(2,1)} %fusion) | data formatting | bytes 14680064
  262.8 14.7 %all-gather.9.cloned.1.call-done = bf16[512,1792]{1,0:T(8,128)(2,1)} async-done(((bf16[256,1792]{1,0:T(8,128)(2,1)}), bf16[512,1792]{1,0:T(8,128)(2,1)}) %all-gather.9.cloned.1.call-update) | async-done | bytes 1835024 | tf_op jit(solution)/shard_map/all_gather | solution.py:65
  277.5 7.6 %fusion.1 = bf16[2048,1792]{0,1:T(8,128)(2,1)} fusion(bf16[512,1792]{1,0:T(8,128)(2,1)} %all-gather.9.cloned.1.call-done, bf16[512,2048]{1,0:T(8,128)(2,1)S(1)} %copy-done.3), kind=kOutput, calls=%fused_computation.5 | convolution fusion | flops 3761766400 | bytes 11272192 | tf_op jit(solution)/shard_map/dot_general | solution.py:30
  285.1 0.0 copy-start
  285.1 10.2 %copy.9 = bf16[2048,1792]{1,0:T(8,128)(2,1)} copy(bf16[2048,1792]{0,1:T(8,128)(2,1)} %fusion.1) | data formatting | bytes 14680064
  295.2 13.9 %all-gather.11.cloned.1.call-done = bf16[512,1792]{1,0:T(8,128)(2,1)} async-done(((bf16[256,1792]{1,0:T(8,128)(2,1)}), bf16[512,1792]{1,0:T(8,128)(2,1)}) %all-gather.11.cloned.1.call-update) | async-done | bytes 1835024 | tf_op jit(solution)/shard_map/all_gather | solution.py:63
  309.2 0.0 copy-done
  309.2 7.6 %convolution_convert_fusion = bf16[1792,2048]{1,0:T(8,128)(2,1)} fusion(bf16[512,1792]{1,0:T(8,128)(2,1)} %all-gather.11.cloned.1.call-done, bf16[512,2048]{1,0:T(8,128)(2,1)S(1)} %bitcast.36), kind=kOutput, calls=%fused_computation.1 | convolution fusion | flops 3761766400 | bytes 11272192 | tf_op jit(solution)/shard_map/dot_general | solution.py:30
  (8 shorter events, 0.1 us)
Async XLA Ops:
  8.0 38.9 %copy-start.1 = (bf16[64,2048]{1,0:T(8,128)(2,1)S(1)}, bf16[64,2048]{1,0:T(8,128)(2,1)}, u32[]{:S(2)}) copy-start(bf16[64,2048]{1,0:T(8,128)(2,1)} %param.6) | copy-start | bytes 786436
  8.0 59.3 %all-gather.5.cloned.1.call-start = ((), (), s32[]{:S(2)}) async-start(), calls=%async_computation.4 | async-start | bytes 2359296 | tf_op jit(solution)/shard_map/all_gather | solution.py:48
  8.1 8.8 %collective-permute-start = (bf16[64,2048]{1,0:T(8,128)(2,1)}, bf16[64,2048]{1,0:T(8,128)(2,1)S(1)}, u32[]{:S(2)}, u32[]{:S(2)}) collective-permute-start(bf16[64,2048]{1,0:T(8,128)(2,1)} %param.6), channel_id=1, source_target_pairs={{0,2},{2,4},{4,6},{6,8},{8,10},{10,12},{12,14},{14,0},{1,3},{3,5},... | collective-permute-start | bytes 786440 | tf_op jit(solution)/shard_map/ppermute | solution.py:20
  16.9 9.5 %collective-permute-start.1 = (bf16[64,2048]{1,0:T(8,128)(2,1)S(1)}, bf16[64,2048]{1,0:T(8,128)(2,1)S(1)}, u32[]{:S(2)}, u32[]{:S(2)}) collective-permute-start(bf16[64,2048]{1,0:T(8,128)(2,1)S(1)} %collective-permute-done), channel_id=1, source_target_pairs={{0,2},{2,4},{4,6},{6,8},{8,10},{10,12},{12,14},{14,0},{1,3},{3,5},... | collective-permute-start | bytes 786440 | tf_op jit(solution)/shard_map/ppermute | solution.py:20
  16.9 9.5 %collective-permute-start.4 = (bf16[64,2048]{1,0:T(8,128)(2,1)}, bf16[64,2048]{1,0:T(8,128)(2,1)S(1)}, u32[]{:S(2)}, u32[]{:S(2)}) collective-permute-start(bf16[64,2048]{1,0:T(8,128)(2,1)} %param.6), channel_id=1, source_target_pairs={{2,0},{4,2},{6,4},{8,6},{10,8},{12,10},{14,12},{0,14},{3,1},{5,3},... | collective-permute-start | bytes 786440 | tf_op jit(solution)/shard_map/ppermute | solution.py:22
  26.3 9.9 %collective-permute-start.2 = (bf16[64,2048]{1,0:T(8,128)(2,1)S(1)}, bf16[64,2048]{1,0:T(8,128)(2,1)S(1)}, u32[]{:S(2)}, u32[]{:S(2)}) collective-permute-start(bf16[64,2048]{1,0:T(8,128)(2,1)S(1)} %collective-permute-done.1), channel_id=1, source_target_pairs={{0,2},{2,4},{4,6},{6,8},{8,10},{10,12},{12,14},{14,0},{1,3},{3,5},... | collective-permute-start | bytes 786440 | tf_op jit(solution)/shard_map/ppermute | solution.py:20
  26.4 10.0 %collective-permute-start.5 = (bf16[64,2048]{1,0:T(8,128)(2,1)S(1)}, bf16[64,2048]{1,0:T(8,128)(2,1)S(1)}, u32[]{:S(2)}, u32[]{:S(2)}) collective-permute-start(bf16[64,2048]{1,0:T(8,128)(2,1)S(1)} %collective-permute-done.4), channel_id=1, source_target_pairs={{2,0},{4,2},{6,4},{8,6},{10,8},{12,10},{14,12},{0,14},{3,1},{5,3},... | collective-permute-start | bytes 786440 | tf_op jit(solution)/shard_map/ppermute | solution.py:22
  36.2 3.7 %copy-start.2 = (bf16[64,2048]{1,0:T(8,128)(2,1)}, bf16[64,2048]{1,0:T(8,128)(2,1)S(1)}, u32[]{:S(2)}) copy-start(bf16[64,2048]{1,0:T(8,128)(2,1)S(1)} %collective-permute-done.2) | copy-start | bytes 786436
  36.2 8.6 %collective-permute-start.3 = (bf16[64,2048]{1,0:T(8,128)(2,1)S(1)}, bf16[64,2048]{1,0:T(8,128)(2,1)}, u32[]{:S(2)}, u32[]{:S(2)}) collective-permute-start(bf16[64,2048]{1,0:T(8,128)(2,1)S(1)} %collective-permute-done.2), channel_id=1, source_target_pairs={{0,2},{2,4},{4,6},{6,8},{8,10},{10,12},{12,14},{14,0},{1,3},{3,5},... | collective-permute-start | bytes 786440 | tf_op jit(solution)/shard_map/ppermute | solution.py:20
  36.2 70.3 %reduce-scatter.4.cloned.1.call-start = ((), (), s32[]{:S(2)}) async-start(), calls=%async_computation.3 | async-start | bytes 5505024 | tf_op jit(solution)/shard_map/reduce_scatter | solution.py:60
  36.3 10.6 %collective-permute-start.6 = (bf16[64,2048]{1,0:T(8,128)(2,1)S(1)}, bf16[64,2048]{1,0:T(8,128)(2,1)S(1)}, u32[]{:S(2)}, u32[]{:S(2)}) collective-permute-start(bf16[64,2048]{1,0:T(8,128)(2,1)S(1)} %collective-permute-done.5), channel_id=1, source_target_pairs={{2,0},{4,2},{6,4},{8,6},{10,8},{12,10},{14,12},{0,14},{3,1},{5,3},... | collective-permute-start | bytes 786440 | tf_op jit(solution)/shard_map/ppermute | solution.py:22
  58.7 99.7 %reduce-scatter.6.cloned.1.call-start = ((), (), s32[]{:S(2)}) async-start(), calls=%async_computation.5 | async-start | bytes 5505024 | tf_op jit(solution)/shard_map/reduce_scatter | solution.py:58
  76.8 1.7 copy-start.3
  76.8 133.3 %reduce-scatter.8.cloned.1.call-start = ((), (), s32[]{:S(2)}) async-start(), calls=%async_computation.6 | async-start | bytes 5505024 | tf_op jit(solution)/shard_map/reduce_scatter | solution.py:57
  87.4 157.9 %all-gather.7.cloned.1.call-start = ((), (), s32[]{:S(2)}) async-start(), calls=%async_computation.7 | async-start | bytes 2752512 | tf_op jit(solution)/shard_map/all_gather | solution.py:64
  215.1 62.4 %all-gather.9.cloned.1.call-start = ((), (), s32[]{:S(2)}) async-start(), calls=%async_computation.8 | async-start | bytes 2752512 | tf_op jit(solution)/shard_map/all_gather | solution.py:65
  215.9 93.3 %all-gather.11.cloned.1.call-start = ((), (), s32[]{:S(2)}) async-start(), calls=%async_computation.9 | async-start | bytes 2752512 | tf_op jit(solution)/shard_map/all_gather | solution.py:63
  285.1 24.1 %copy-start = (bf16[8,64,2048]{2,1,0:T(8,128)(2,1)S(1)}, bf16[8,64,2048]{2,1,0:T(8,128)(2,1)}, u32[]{:S(2)}) copy-start(bf16[8,64,2048]{2,1,0:T(8,128)(2,1)} %gather_fusion) | copy-start | bytes 6291460
Sparse Core Ops, SparseCore 0:
  36.4 30.8 all-gather.4
Sparse Core Ops, SparseCore 1:
  58.8 47.7 reduce-scatter.3
  109.3 49.0 reduce-scatter.5
  161.1 49.0 reduce-scatter.7
  215.2 30.0 all-gather.6
  247.5 30.0 all-gather.8
  279.1 30.0 all-gather.10
